TPU v7x, 32 devices: a whole 2x2x4 slice. The times are simulated.
32 devices in a mesh: dom: 2 (over y), rep: 4 (over z), tp: 4 (over x, core).
Axes of the slice: x: 2, y: 2, z: 4, core: 2. Of those that a mesh axis runs over, the one named last changes fastest.
Arguments:
- normed_hidden: bfloat16 [4, 1536, 8192], P(None, ('dom', 'rep'), 'tp'), parts along dimension 1, may hold values from -6 to 6
- key_weight_base: bfloat16 [8192, 1024], P('tp'), may hold values from -0.0625 to 0.0625
- adapter_down_factors: bfloat16 [256, 64, 8192], P('rep', None, 'tp'), may hold values from -0.0625 to 0.0625
- adapter_up_factors: bfloat16 [256, 64, 1024], P('rep', None, 'tp'), may hold values from -0.75 to 0.75
- request_adapter: int32 [1536], P(('dom', 'rep')), parts along dimension 0, may hold values from 0 to 255, as said below
- adapter_position: int32 [512], P('dom'), parts along dimension 0, may hold values from 0 to 255, as said below
Outputs:
- keys: bfloat16 [4, 1536, 1024], P(None, ('dom', 'rep'), 'tp'), parts along dimension 1
There are 2 independent parts, one for each index of `dom`. A program takes and returns all parts, laid end to end along the dimension named above; an argument that names none is the same for every part. Nothing has to cross between parts.
Inputs may be any that keep to these rules, and one draw needn't show every extreme that they name: `adapter_position`: A permutation; the factors of storage position p lie on the replica of index p // (256 // 4). `request_adapter`: among the 192 requests of one replica, at most 96 use adapters stored on any one replica.
All inputs are finite; a program needn't handle non-finite values.
Results may differ from a plain program's by a relative error of at most 0.001.
Values may be sent and summed in bfloat16 or wider, within the bound.
A program may use at most 128 MiB of HBM per device.

v0:
```python
import functools

import jax
import jax.numpy as jnp
from jax import lax
from jax.experimental import pallas as pl
from jax.experimental.pallas import tpu as pltpu
from jax.sharding import PartitionSpec as P

MESH = pl.DeviceIdType.MESH
F32 = jnp.float32
BF16 = jnp.bfloat16


def split_two(value):
    high = value.astype(BF16)
    low = (value - high.astype(F32)).astype(BF16)
    return high, low


def iota(shape, dim):
    return lax.broadcasted_iota(jnp.int32, shape, dim)


def kernel(
    dims,
    x_hbm,
    w_hbm,
    down_hbm,
    up_hbm,
    ra_col,
    ra_row,
    ap_col,
    ap_row,
    out,
    x,
    w,
    down,
    up,
    send,
    recv,
    flipped,
    lab_send,
    lab_recv,
    red,
    upd_send,
    upd_recv,
    part,
    rs_recv,
    x_sem,
    load_sem,
    own_sem,
    lab_ssem,
    lab_rsem,
    in_ssem,
    in_rsem,
    red_ssem,
    red_rsem,
    upd_ssem,
    upd_rsem,
    rs_ssem,
    rs_rsem,
):
    reps, tps, steps, rows, cap, grouped, rank = dims
    slots = reps * cap
    width = x.shape[1]
    cols = out.shape[1]
    me = lax.axis_index("rep")
    mt = lax.axis_index("tp")

    def others(count, mine, fn):
        def body(k, carry):
            fn(lax.rem(mine + k, count))
            return carry

        lax.fori_loop(1, count, body, 0)

    def over(count, fn):
        def body(k, carry):
            fn(k)
            return carry

        lax.fori_loop(0, count, body, 0)

    x_loads = [
        pltpu.make_async_copy(
            x_hbm.at[pl.ds(s * rows, rows)], x.at[pl.ds(s * rows, rows)], x_sem.at[s]
        )
        for s in range(steps)
    ]
    for load in x_loads:
        load.start()
    w_load = pltpu.make_async_copy(w_hbm, w, load_sem.at[0])
    down_load = pltpu.make_async_copy(down_hbm, down, load_sem.at[1])
    up_load = pltpu.make_async_copy(up_hbm, up, load_sem.at[2])
    w_load.start()
    down_load.start()
    up_load.start()

    barrier = pltpu.get_barrier_semaphore()
    others(
        reps,
        me,
        lambda d: pl.semaphore_signal(barrier, inc=1, device_id={"rep": d}, device_id_type=MESH),
    )
    others(
        tps,
        mt,
        lambda t: pl.semaphore_signal(barrier, inc=1, device_id={"tp": t}, device_id_type=MESH),
    )

    adapters = ap_row.shape[1]
    pos_col = jnp.sum(
        jnp.where(ra_col[...] == iota((rows, adapters), 1), ap_row[...], 0), axis=1, keepdims=True
    )
    pos_row = jnp.sum(
        jnp.where(ra_row[...] == iota((adapters, rows), 0), ap_col[...], 0), axis=0, keepdims=True
    )
    own_col, own_row = lax.div(pos_col, grouped), lax.div(pos_row, grouped)
    same = own_col == own_row
    sub, lane = iota((rows, rows), 0), iota((rows, rows), 1)
    rank_col = jnp.sum(jnp.where(same & (lane < sub), 1, 0), axis=1, keepdims=True)
    rank_row = jnp.sum(jnp.where(same & (sub < lane), 1, 0), axis=0, keepdims=True)
    target_col = own_col * cap + rank_col
    target_row = own_row * cap + rank_row
    landing = target_row == iota((slots, rows), 0)
    pick = jnp.where(landing, 1.0, 0.0).astype(BF16)
    within = pos_row - own_row * grouped
    label = jnp.sum(jnp.where(landing, within + 1, 0), axis=1, keepdims=True) - 1
    lab_send[...] = jnp.broadcast_to(label, (slots, 128)).astype(F32).reshape(reps, cap, 128)

    pl.semaphore_wait(barrier, reps + tps - 2)

    def lab_copy(there, src):
        return pltpu.make_async_remote_copy(
            src_ref=lab_send.at[there],
            dst_ref=lab_recv.at[src],
            send_sem=lab_ssem.at[there],
            recv_sem=lab_rsem.at[src],
            device_id={"rep": there},
            device_id_type=MESH,
        )

    def in_copy(s, there, src):
        return pltpu.make_async_remote_copy(
            src_ref=send.at[s, there],
            dst_ref=recv.at[s, src],
            send_sem=in_ssem.at[s, there],
            recv_sem=in_rsem.at[s, src],
            device_id={"rep": there},
            device_id_type=MESH,
        )

    def own_copy(s):
        return pltpu.make_async_copy(send.at[s, me], recv.at[s, me], own_sem.at[s])

    def red_copy(s, there, src):
        return pltpu.make_async_remote_copy(
            src_ref=red.at[s, mt],
            dst_ref=red.at[s, src],
            send_sem=red_ssem.at[s, there],
            recv_sem=red_rsem.at[s, src],
            device_id={"tp": there},
            device_id_type=MESH,
        )

    def upd_copy(s, there, src):
        return pltpu.make_async_remote_copy(
            src_ref=upd_send.at[s, there],
            dst_ref=upd_recv.at[s, src],
            send_sem=upd_ssem.at[s, there],
            recv_sem=upd_rsem.at[s, src],
            device_id={"rep": there},
            device_id_type=MESH,
        )

    def rs_copy(there, src):
        return pltpu.make_async_remote_copy(
            src_ref=part.at[there],
            dst_ref=rs_recv.at[src],
            send_sem=rs_ssem.at[there],
            recv_sem=rs_rsem.at[src],
            device_id={"tp": there},
            device_id_type=MESH,
        )

    others(reps, me, lambda d: lab_copy(d, me).start())
    lab_own = pltpu.make_async_copy(lab_send.at[me], lab_recv.at[me], load_sem.at[3])
    lab_own.start()
    chunk = 512
    for s in range(steps):
        x_loads[s].wait()

        def place(c, s=s):
            at = pl.ds(pl.multiple_of(c * chunk, chunk), chunk)
            piece = jnp.dot(
                pick, x[s * rows : (s + 1) * rows, at], preferred_element_type=F32
            )
            send[s, :, :, at] = piece.astype(BF16).reshape(reps, cap, chunk)

        over(width // chunk, place)
        others(reps, me, lambda d, s=s: in_copy(s, d, me).start())
        own_copy(s).start()

    w_load.wait()

    def base_block(t):
        at = pl.ds(pl.multiple_of(t * cols, cols), cols)
        part[t] = jnp.dot(x[...], w[:, at], preferred_element_type=F32)

    def base_send(t):
        base_block(t)
        rs_copy(t, mt).start()

    others(tps, mt, base_send)
    base_block(mt)

    down_load.wait()
    up_load.wait()
    lab_own.wait()
    others(reps, me, lambda d: lab_copy(me, d).wait_recv())
    lab_flat = lab_recv[...].reshape(slots, 128)
    lab_row = jnp.transpose(lab_flat)[0:1, :].astype(jnp.int32)
    lab_col = lab_flat[:, 0:1].astype(jnp.int32)

    block = min(8, grouped)
    wide = max(1, 256 // rank)
    wide = min(wide, grouped)

    def step(s):
        own_copy(s).wait()
        others(reps, me, lambda d: in_copy(s, me, d).wait_recv())
        flipped[...] = jnp.transpose(recv[s].reshape(slots, width))

        def shrink_block(b, acc):
            at = pl.ds(pl.multiple_of(b * block * rank, block * rank), block * rank)
            y = jnp.dot(down[at, :], flipped[...], preferred_element_type=F32)
            for i in range(block):
                acc = jnp.where(
                    lab_row == b * block + i, y[i * rank : (i + 1) * rank, :], acc
                )
            return acc

        red[s, mt] = lax.fori_loop(
            0, grouped // block, shrink_block, jnp.zeros((rank, slots), F32)
        )
        others(tps, mt, lambda t: red_copy(s, t, mt).start())
        others(tps, mt, lambda t: red_copy(s, mt, t).wait_recv())
        total = red[s, 0]
        for t in range(1, tps):
            total = total + red[s, t]
        mine = jnp.transpose(total)
        high = mine.astype(BF16).astype(F32)
        low = mine - high
        high = jnp.concatenate([high] * wide, axis=1)
        low = jnp.concatenate([low] * wide, axis=1)
        group = lax.div(iota((slots, wide * rank), 1), rank)

        def expand_block(g, acc):
            at = pl.ds(pl.multiple_of(g * wide * rank, wide * rank), wide * rank)
            here = (lab_col - g * wide) == group
            some = up[at, :]
            acc = acc + jnp.dot(
                jnp.where(here, high, 0.0).astype(BF16), some, preferred_element_type=F32
            )
            return acc + jnp.dot(
                jnp.where(here, low, 0.0).astype(BF16), some, preferred_element_type=F32
            )

        updates = lax.fori_loop(
            0, grouped // wide, expand_block, jnp.zeros((slots, cols), F32)
        )
        upd_send[s] = updates.reshape(reps, cap, cols)
        upd_recv[s, me] = upd_send[s, me]
        others(reps, me, lambda d: upd_copy(s, d, me).start())

    over(steps, step)

    others(tps, mt, lambda t: rs_copy(mt, t).wait_recv())
    take = jnp.where(target_col == iota((rows, slots), 1), 1.0, 0.0).astype(BF16)

    def finish(s):
        at = pl.ds(pl.multiple_of(s * rows, rows), rows)
        total = part[mt, at, :]

        def add(k, total):
            return total + rs_recv[lax.rem(mt + k, tps), at, :]

        total = lax.fori_loop(1, tps, add, total)
        others(reps, me, lambda d: upd_copy(s, me, d).wait_recv())
        high, low = split_two(upd_recv[s].reshape(slots, cols))
        deltas = jnp.dot(take, high, preferred_element_type=F32) + jnp.dot(
            take, low, preferred_element_type=F32
        )
        out[at, :] = (total + deltas).astype(BF16)

    over(steps, finish)

    others(reps, me, lambda d: lab_copy(d, me).wait_send())
    others(tps, mt, lambda t: rs_copy(t, mt).wait_send())

    def drain(s):
        others(reps, me, lambda d: in_copy(s, d, me).wait_send())
        others(tps, mt, lambda t: red_copy(s, t, mt).wait_send())
        others(reps, me, lambda d: upd_copy(s, d, me).wait_send())

    over(steps, drain)


def local(x, w, down, up, request_adapter, adapter_position):
    steps, rows, width = x.shape
    reps, tps = lax.axis_size("rep"), lax.axis_size("tp")
    grouped, rank, _ = down.shape
    cols = up.shape[2]
    cap = -(-(2 * rows // reps) // 16) * 16
    slots = reps * cap
    adapters = adapter_position.shape[0]
    any_spec = pl.BlockSpec(memory_space=pl.ANY)
    vmem_spec = pl.BlockSpec(memory_space=pltpu.VMEM)
    dma = pltpu.SemaphoreType.DMA
    dims = (reps, tps, steps, rows, cap, grouped, rank)
    keys = pl.pallas_call(
        functools.partial(kernel, dims),
        out_shape=jax.ShapeDtypeStruct((steps * rows, cols), BF16),
        in_specs=[any_spec] * 4 + [vmem_spec] * 4,
        out_specs=vmem_spec,
        scratch_shapes=[
            pltpu.VMEM((steps * rows, width), BF16),
            pltpu.VMEM(w.shape, BF16),
            pltpu.VMEM((grouped * rank, width), BF16),
            pltpu.VMEM((grouped * rank, cols), BF16),
            pltpu.VMEM((steps, reps, cap, width), BF16),
            pltpu.VMEM((steps, reps, cap, width), BF16),
            pltpu.VMEM((width, slots), BF16),
            pltpu.VMEM((reps, cap, 128), F32),
            pltpu.VMEM((reps, cap, 128), F32),
            pltpu.VMEM((steps, tps, rank, slots), F32),
            pltpu.VMEM((steps, reps, cap, cols), F32),
            pltpu.VMEM((steps, reps, cap, cols), F32),
            pltpu.VMEM((tps, steps * rows, cols), F32),
            pltpu.VMEM((tps, steps * rows, cols), F32),
            dma((steps,)),
            dma((4,)),
            dma((steps,)),
            dma((reps,)),
            dma((reps,)),
            dma((steps, reps)),
            dma((steps, reps)),
            dma((steps, tps)),
            dma((steps, tps)),
            dma((steps, reps)),
            dma((steps, reps)),
            dma((tps,)),
            dma((tps,)),
        ],
        compiler_params=pltpu.CompilerParams(
            collective_id=0, has_side_effects=True, vmem_limit_bytes=62 * 1024 * 1024
        ),
        cost_estimate=pl.CostEstimate(
            flops=2 * steps * slots * grouped * rank * width,
            bytes_accessed=2 * grouped * rank * width,
            transcendentals=0,
        ),
    )(
        x.reshape(steps * rows, width),
        w,
        down.reshape(grouped * rank, width),
        up.reshape(grouped * rank, cols),
        request_adapter.reshape(rows, 1),
        request_adapter.reshape(1, rows),
        adapter_position.reshape(adapters, 1),
        adapter_position.reshape(1, adapters),
    )
    return keys.reshape(steps, rows, cols)


def solution(mesh):
    return jax.shard_map(
        local,
        mesh=mesh,
        in_specs=(
            P(None, ("dom", "rep"), "tp"),
            P("tp", None),
            P("rep", None, "tp"),
            P("rep", None, "tp"),
            P(("dom", "rep")),
            P("dom"),
        ),
        out_specs=P(None, ("dom", "rep"), "tp"),
        check_vma=False,
    )
```

profile of v0, /device:TPU:17, one launch (start us, length us, event | category | flops | bytes accessed | tf_op | source)
XLA Modules:
  0.0 194.4 jit_solution(9746888834551647433)
XLA Ops:
  0.0 1.4 copy.7.ra_col
  1.4 1.5 copy.8.ap_col
  2.9 189.8 %shard_map.64 = bf16[768,256]{1,0:T(8,128)(2,1)} custom-call(bf16[768,2048]{1,0:T(8,128)(2,1)} %bitcast.14, bf16[2048,1024]{1,0:T(8,128)(2,1)} %w_hbm.1, bf16[4096,2048]{1,0:T(8,128)(2,1)} %bitcast.13, bf16[4096,256]{1,0:T(8,128)(2,1)} %bitcast.15, s32[192,1]{1,0:T(8,128)} %copy.7.ra_col, s32[1,192]{1,0:T(1,128)} %bitcast.10, s32[256,1]{1,0:T(8,128)} %copy.8.ap_col, ...), custom_call_target="tpu_custom_call" | custom-call | flops 25769803776 | bytes 16777216 | tf_op jit(solution)/shard_map/pallas_call | solution.py:322
  192.7 1.8 copy.10
where the time goes:
time: 195 us; the launch traced here: 194 us
  Pallas kernels  190 us (97%)
  local copies, waits for them, and re-layouts  4.67 us (2%)
    pallas_call x1, Pallas kernels, local(): pl.pallas_call(functools.partial(kernel, dims), out_shape=jax.ShapeDtypeS...  190 us

commit v1 on v0

--- a/solution.py
+++ b/solution.py
@@ -28,9 +28,7 @@
     w_hbm,
     down_hbm,
     up_hbm,
-    ra_col,
     ra_row,
-    ap_col,
     ap_row,
     out,
     x,
@@ -42,6 +40,7 @@
     flipped,
     lab_send,
     lab_recv,
+    lab_rows,
     red,
     upd_send,
     upd_recv,
@@ -61,8 +60,10 @@
     rs_ssem,
     rs_rsem,
 ):
-    reps, tps, steps, rows, cap, grouped, rank = dims
-    slots = reps * cap
+    reps, tps, steps, rows, cap, halves, grouped, rank = dims
+    hcap = cap // halves
+    slots = reps * hcap
+    chunks = steps * halves
     width = x.shape[1]
     cols = out.shape[1]
     me = lax.axis_index("rep")
@@ -110,33 +111,42 @@
     )
 
     adapters = ap_row.shape[1]
-    pos_col = jnp.sum(
-        jnp.where(ra_col[...] == iota((rows, adapters), 1), ap_row[...], 0), axis=1, keepdims=True
-    )
+
+    def column(row):
+        n = row.shape[1]
+        return jnp.sum(
+            jnp.where(iota((n, n), 0) == iota((n, n), 1), row, 0), axis=1, keepdims=True
+        )
+
+    ap_col = column(ap_row[...])
     pos_row = jnp.sum(
-        jnp.where(ra_row[...] == iota((adapters, rows), 0), ap_col[...], 0), axis=0, keepdims=True
-    )
+        jnp.where(ra_row[...] == iota((adapters, rows), 0), ap_col, 0), axis=0, keepdims=True
+    )
+    pos_col = column(pos_row)
     own_col, own_row = lax.div(pos_col, grouped), lax.div(pos_row, grouped)
     same = own_col == own_row
     sub, lane = iota((rows, rows), 0), iota((rows, rows), 1)
     rank_col = jnp.sum(jnp.where(same & (lane < sub), 1, 0), axis=1, keepdims=True)
     rank_row = jnp.sum(jnp.where(same & (sub < lane), 1, 0), axis=0, keepdims=True)
-    target_col = own_col * cap + rank_col
-    target_row = own_row * cap + rank_row
-    landing = target_row == iota((slots, rows), 0)
+    half_col, half_row = lax.div(rank_col, hcap), lax.div(rank_row, hcap)
+    target_col = half_col * slots + own_col * hcap + (rank_col - half_col * hcap)
+    target_row = half_row * slots + own_row * hcap + (rank_row - half_row * hcap)
+    landing = target_row == iota((halves * slots, rows), 0)
     pick = jnp.where(landing, 1.0, 0.0).astype(BF16)
     within = pos_row - own_row * grouped
     label = jnp.sum(jnp.where(landing, within + 1, 0), axis=1, keepdims=True) - 1
-    lab_send[...] = jnp.broadcast_to(label, (slots, 128)).astype(F32).reshape(reps, cap, 128)
+    lab_send[...] = jnp.broadcast_to(label.astype(F32), (halves * slots, 128)).reshape(
+        halves, reps, hcap, 128
+    )
 
     pl.semaphore_wait(barrier, reps + tps - 2)
 
-    def lab_copy(there, src):
+    def lab_copy(h, there, src):
         return pltpu.make_async_remote_copy(
-            src_ref=lab_send.at[there],
-            dst_ref=lab_recv.at[src],
-            send_sem=lab_ssem.at[there],
-            recv_sem=lab_rsem.at[src],
+            src_ref=lab_send.at[h, there],
+            dst_ref=lab_recv.at[h, src],
+            send_sem=lab_ssem.at[h, there],
+            recv_sem=lab_rsem.at[h, src],
             device_id={"rep": there},
             device_id_type=MESH,
         )
@@ -184,23 +194,27 @@
             device_id_type=MESH,
         )
 
-    others(reps, me, lambda d: lab_copy(d, me).start())
-    lab_own = pltpu.make_async_copy(lab_send.at[me], lab_recv.at[me], load_sem.at[3])
-    lab_own.start()
+    for h in range(halves):
+        others(reps, me, lambda d, h=h: lab_copy(h, d, me).start())
+        lab_recv[h, me] = lab_send[h, me]
     chunk = 512
     for s in range(steps):
         x_loads[s].wait()
 
-        def place(c, s=s):
-            at = pl.ds(pl.multiple_of(c * chunk, chunk), chunk)
-            piece = jnp.dot(
-                pick, x[s * rows : (s + 1) * rows, at], preferred_element_type=F32
-            )
-            send[s, :, :, at] = piece.astype(BF16).reshape(reps, cap, chunk)
-
-        over(width // chunk, place)
-        others(reps, me, lambda d, s=s: in_copy(s, d, me).start())
-        own_copy(s).start()
+        for h in range(halves):
+
+            def place(c, s=s, h=h):
+                at = pl.ds(pl.multiple_of(c * chunk, chunk), chunk)
+                piece = jnp.dot(
+                    pick[h * slots : (h + 1) * slots],
+                    x[s * rows : (s + 1) * rows, at],
+                    preferred_element_type=F32,
+                )
+                send[s * halves + h, :, :, at] = piece.astype(BF16).reshape(reps, hcap, chunk)
+
+            over(width // chunk, place)
+            others(reps, me, lambda d, q=s * halves + h: in_copy(q, d, me).start())
+            own_copy(s * halves + h).start()
 
     w_load.wait()
 
@@ -217,17 +231,19 @@
 
     down_load.wait()
     up_load.wait()
-    lab_own.wait()
-    others(reps, me, lambda d: lab_copy(me, d).wait_recv())
-    lab_flat = lab_recv[...].reshape(slots, 128)
-    lab_row = jnp.transpose(lab_flat)[0:1, :].astype(jnp.int32)
-    lab_col = lab_flat[:, 0:1].astype(jnp.int32)
+    for h in range(halves):
+        others(reps, me, lambda d, h=h: lab_copy(h, me, d).wait_recv())
+        flat = lab_recv[h].reshape(slots, 128)
+        lab_rows[h] = jnp.transpose(flat)[0:8, :].astype(jnp.int32)
 
     block = min(8, grouped)
     wide = max(1, 256 // rank)
     wide = min(wide, grouped)
 
     def step(s):
+        h = lax.rem(s, halves)
+        lab_row = lab_rows[h][0:1, :]
+        lab_col = lab_recv[h].reshape(slots, 128)[:, 0:1].astype(jnp.int32)
         own_copy(s).wait()
         others(reps, me, lambda d: in_copy(s, me, d).wait_recv())
         flipped[...] = jnp.transpose(recv[s].reshape(slots, width))
@@ -270,14 +286,14 @@
         updates = lax.fori_loop(
             0, grouped // wide, expand_block, jnp.zeros((slots, cols), F32)
         )
-        upd_send[s] = updates.reshape(reps, cap, cols)
+        upd_send[s] = updates.reshape(reps, hcap, cols)
         upd_recv[s, me] = upd_send[s, me]
         others(reps, me, lambda d: upd_copy(s, d, me).start())
 
-    over(steps, step)
+    over(chunks, step)
 
     others(tps, mt, lambda t: rs_copy(mt, t).wait_recv())
-    take = jnp.where(target_col == iota((rows, slots), 1), 1.0, 0.0).astype(BF16)
+    take = jnp.where(target_col == iota((rows, halves * slots), 1), 1.0, 0.0).astype(BF16)
 
     def finish(s):
         at = pl.ds(pl.multiple_of(s * rows, rows), rows)
@@ -287,16 +303,19 @@
             return total + rs_recv[lax.rem(mt + k, tps), at, :]
 
         total = lax.fori_loop(1, tps, add, total)
-        others(reps, me, lambda d: upd_copy(s, me, d).wait_recv())
-        high, low = split_two(upd_recv[s].reshape(slots, cols))
-        deltas = jnp.dot(take, high, preferred_element_type=F32) + jnp.dot(
-            take, low, preferred_element_type=F32
-        )
-        out[at, :] = (total + deltas).astype(BF16)
+        for h in range(halves):
+            q = s * halves + h
+            others(reps, me, lambda d, q=q: upd_copy(q, me, d).wait_recv())
+            high, low = split_two(upd_recv[q].reshape(slots, cols))
+            mine = take[:, h * slots : (h + 1) * slots]
+            total = total + jnp.dot(mine, high, preferred_element_type=F32)
+            total = total + jnp.dot(mine, low, preferred_element_type=F32)
+        out[at, :] = total.astype(BF16)
 
     over(steps, finish)
 
-    others(reps, me, lambda d: lab_copy(d, me).wait_send())
+    for h in range(halves):
+        others(reps, me, lambda d, h=h: lab_copy(h, d, me).wait_send())
     others(tps, mt, lambda t: rs_copy(t, mt).wait_send())
 
     def drain(s):
@@ -304,7 +323,7 @@
         others(tps, mt, lambda t: red_copy(s, t, mt).wait_send())
         others(reps, me, lambda d: upd_copy(s, d, me).wait_send())
 
-    over(steps, drain)
+    over(chunks, drain)
 
 
 def local(x, w, down, up, request_adapter, adapter_position):
@@ -313,43 +332,47 @@
     grouped, rank, _ = down.shape
     cols = up.shape[2]
     cap = -(-(2 * rows // reps) // 16) * 16
-    slots = reps * cap
+    halves = 2 if cap % 32 == 0 else 1
+    hcap = cap // halves
+    slots = reps * hcap
+    chunks = steps * halves
     adapters = adapter_position.shape[0]
     any_spec = pl.BlockSpec(memory_space=pl.ANY)
     vmem_spec = pl.BlockSpec(memory_space=pltpu.VMEM)
     dma = pltpu.SemaphoreType.DMA
-    dims = (reps, tps, steps, rows, cap, grouped, rank)
+    dims = (reps, tps, steps, rows, cap, halves, grouped, rank)
     keys = pl.pallas_call(
         functools.partial(kernel, dims),
         out_shape=jax.ShapeDtypeStruct((steps * rows, cols), BF16),
-        in_specs=[any_spec] * 4 + [vmem_spec] * 4,
+        in_specs=[any_spec] * 4 + [vmem_spec] * 2,
         out_specs=vmem_spec,
         scratch_shapes=[
             pltpu.VMEM((steps * rows, width), BF16),
             pltpu.VMEM(w.shape, BF16),
             pltpu.VMEM((grouped * rank, width), BF16),
             pltpu.VMEM((grouped * rank, cols), BF16),
-            pltpu.VMEM((steps, reps, cap, width), BF16),
-            pltpu.VMEM((steps, reps, cap, width), BF16),
+            pltpu.VMEM((chunks, reps, hcap, width), BF16),
+            pltpu.VMEM((chunks, reps, hcap, width), BF16),
             pltpu.VMEM((width, slots), BF16),
-            pltpu.VMEM((reps, cap, 128), F32),
-            pltpu.VMEM((reps, cap, 128), F32),
-            pltpu.VMEM((steps, tps, rank, slots), F32),
-            pltpu.VMEM((steps, reps, cap, cols), F32),
-            pltpu.VMEM((steps, reps, cap, cols), F32),
+            pltpu.VMEM((halves, reps, hcap, 128), F32),
+            pltpu.VMEM((halves, reps, hcap, 128), F32),
+            pltpu.VMEM((halves, 8, slots), jnp.int32),
+            pltpu.VMEM((chunks, tps, rank, slots), F32),
+            pltpu.VMEM((chunks, reps, hcap, cols), F32),
+            pltpu.VMEM((chunks, reps, hcap, cols), F32),
             pltpu.VMEM((tps, steps * rows, cols), F32),
             pltpu.VMEM((tps, steps * rows, cols), F32),
             dma((steps,)),
-            dma((4,)),
-            dma((steps,)),
-            dma((reps,)),
-            dma((reps,)),
-            dma((steps, reps)),
-            dma((steps, reps)),
-            dma((steps, tps)),
-            dma((steps, tps)),
-            dma((steps, reps)),
-            dma((steps, reps)),
+            dma((3,)),
+            dma((chunks,)),
+            dma((halves, reps)),
+            dma((halves, reps)),
+            dma((chunks, reps)),
+            dma((chunks, reps)),
+            dma((chunks, tps)),
+            dma((chunks, tps)),
+            dma((chunks, reps)),
+            dma((chunks, reps)),
             dma((tps,)),
             dma((tps,)),
         ],
@@ -357,7 +380,7 @@
             collective_id=0, has_side_effects=True, vmem_limit_bytes=62 * 1024 * 1024
         ),
         cost_estimate=pl.CostEstimate(
-            flops=2 * steps * slots * grouped * rank * width,
+            flops=2 * chunks * slots * grouped * rank * width,
             bytes_accessed=2 * grouped * rank * width,
             transcendentals=0,
         ),
@@ -366,9 +389,7 @@
         w,
         down.reshape(grouped * rank, width),
         up.reshape(grouped * rank, cols),
-        request_adapter.reshape(rows, 1),
         request_adapter.reshape(1, rows),
-        adapter_position.reshape(adapters, 1),
         adapter_position.reshape(1, adapters),
     )
     return keys.reshape(steps, rows, cols)

time: 195 us -> 198 us (1.015)
  Pallas kernels: 190 us -> 195 us
  local copies, waits for them, and re-layouts: 4.67 us -> 1.77 us
    pallas_call x1, Pallas kernels: 190 us -> 195 us  [local(): pl.pallas_call(functools.partial(kernel, dims), out_shape=jax.ShapeDtypeS...]
    reshape x2 -> x0, local copies, waits for them, and re-layouts: 2.9 us -> none  [the longest x1 1.47 us: local(): adapter_position.reshape(adapters, 1)]
where the time goes in v1:
time: 198 us; the launch traced here: 197 us
  Pallas kernels  195 us (98%)
    pallas_call x1, Pallas kernels, local(): pl.pallas_call(functools.partial(kernel, dims), out_shape=jax.ShapeDtypeS...  195 us

profile of v1, /device:TPU:17, one launch (start us, length us, event | category | flops | bytes accessed | tf_op | source)
XLA Modules:
  0.0 197.2 jit_solution(15082163935374089081)
XLA Ops:
  0.0 195.4 %shard_map.64 = bf16[768,256]{1,0:T(8,128)(2,1)} custom-call(bf16[768,2048]{1,0:T(8,128)(2,1)} %bitcast.8, bf16[2048,1024]{1,0:T(8,128)(2,1)} %w_hbm.1, bf16[4096,2048]{1,0:T(8,128)(2,1)} %bitcast.7, bf16[4096,256]{1,0:T(8,128)(2,1)} %bitcast.9, s32[1,192]{1,0:T(1,128)} %bitcast.10, s32[1,256]{1,0:T(1,128)} %bitcast.11), custom_call_target="tpu_custom_call" | custom-call | flops 25769803776 | bytes 16777216 | tf_op jit(solution)/shard_map/pallas_call | solution.py:344
  195.4 1.8 copy.8
